TPU v7x, 128 devices: a whole 4x4x4 slice. The times are simulated.
128 devices in a mesh: frame: 16 (over y, x), orbit: 8 (over z, core).
Axes of the slice: x: 4, y: 4, z: 4, core: 2. Of those that a mesh axis runs over, the one named last changes fastest.
Arguments:
- tokens: bfloat16 [65536, 1536], P(('orbit', 'frame')), parts along dimension 0, may hold values from -8 to 8
- keep_count: int32 [128], P('orbit'), parts along dimension 0, may hold values from 1 to 3, 32 in all
- keep_order: int32 [128, 4], P(('orbit', 'frame')), parts along dimension 0, may hold values from 0 to 3, each once within a row
- w_qkv: bfloat16 [1536, 4608], replicated, may hold values from -1 to 1
- w_out: bfloat16 [1536, 1536], replicated, may hold values from -0.15625 to 0.15625
Outputs:
- updated: bfloat16 [65536, 1536], P(('orbit', 'frame')), parts along dimension 0
There are 8 independent parts, one for each index of `orbit`. A program takes and returns all parts, laid end to end along the dimension named above; an argument that names none is the same for every part. Nothing has to cross between parts.
Inputs may be any that keep to these rules, and one draw needn't show every extreme that they name: `keep_count`: the counts sum to 32 and some frame keeps exactly 3 blocks. `keep_order`: each row is a permutation of the numbers 0 to 3.
All inputs are finite; a program needn't handle non-finite values.
Results may differ from a plain program's by a relative error of at most 0.0086.
Values may be sent and summed in bfloat16 or wider, within the bound.
A program may use at most 320 MiB of HBM per device.

v0:
```python
import functools

import jax
import jax.numpy as jnp
from jax import lax
from jax.experimental import pallas as pl
from jax.experimental.pallas import tpu as pltpu
from jax.sharding import PartitionSpec as P

D = 1536
HEADS = 24
HEAD_DIM = 64
BLK = 128
MOSTB = 3
ROWS = MOSTB * BLK
SIDE = 4
GW = 384
CH = 1024
WINDOW = 28 * BLK
BEGUN_WINDOW = 16 * BLK
KROWS = 36 * BLK + CH
SCALE = HEAD_DIM ** (-0.5) * 1.4426950408889634
MESH = pl.DeviceIdType.MESH


def place():
    me = lax.axis_index("frame")
    return me // SIDE, me % SIDE


def device(y, x):
    return {"frame": (y % SIDE) * SIDE + x % SIDE}


def norm_kernel(order, tokens, out, kept, sems):
    loads = []
    for j in range(MOSTB):
        rows = pl.ds(pl.multiple_of(order[0, j] * BLK, BLK), BLK)
        loads.append(pltpu.make_async_copy(tokens.at[rows, :], kept.at[j], sems.at[j]))
        loads[j].start()
    for j in range(MOSTB):
        loads[j].wait()
        wide = kept[j].astype(jnp.float32)
        scale = lax.rsqrt(jnp.mean(wide * wide, axis=-1, keepdims=True) + 1e-06)
        out[j * BLK : (j + 1) * BLK, :] = (wide * scale).astype(jnp.bfloat16)


def norm_kept(keep_order, tokens):
    return pl.pallas_call(
        norm_kernel,
        in_specs=[pl.BlockSpec(memory_space=pltpu.SMEM), pl.BlockSpec(memory_space=pltpu.HBM)],
        out_specs=pl.BlockSpec(memory_space=pltpu.VMEM),
        out_shape=jax.ShapeDtypeStruct((ROWS, D), jnp.bfloat16),
        scratch_shapes=[pltpu.VMEM((MOSTB, BLK, D), jnp.bfloat16), pltpu.SemaphoreType.DMA((MOSTB,))],
        compiler_params=pltpu.CompilerParams(vmem_limit_bytes=12 * 2**20),
        name="norm_kept",
    )(keep_order, tokens)


BLOCKS = ((1, 1), (1, 2), (0, 1), (0, 2), (3, 1), (3, 2), (2, 1), (2, 2), (1, 0), (3, 0), (2, 0), (0, 0))
FW = 256
LW = GW - FW


def exchange_kernel(
    keep, normed, w, below, row, above, last, q, tops, sums, wbuf, kvs, lasts, qs,
    wsem, xs, xr, ls, lr, qss, qsr, rss, rsr, ys, yr,
):
    y, x = place()
    loads = []
    for i, (delta, kind) in enumerate(BLOCKS):
        col = pl.multiple_of(kind * (HEADS * HEAD_DIM) + ((x + delta) % SIDE) * GW, 128)
        load = pltpu.make_async_copy(w.at[:, pl.ds(col, GW)], wbuf.at[i], wsem.at[i])
        load.start()
        loads.append(load)
    barrier = pltpu.get_barrier_semaphore()
    peers = [(0, 1), (0, 2), (0, 3), (1, 0), (3, 0)]
    for dy, dx in peers:
        pl.semaphore_signal(barrier, inc=1, device_id=device(y + dy, x + dx), device_id_type=MESH)
    pl.semaphore_wait(barrier, len(peers))

    def product(i, put):
        loads[i].wait()

        def rows(r, carry):
            at = pl.ds(pl.multiple_of(r * BLK, BLK), BLK)
            value = jnp.dot(normed[at, :], wbuf[i], preferred_element_type=jnp.float32)
            put(at, value)
            return carry

        lax.fori_loop(0, MOSTB, rows, 0)

    def across(src, dst, send, recv, delta):
        return pltpu.make_async_remote_copy(
            src.at[delta], dst.at[delta], send.at[delta], recv.at[delta],
            device_id=device(y, x + delta), device_id_type=MESH,
        )

    first = {delta: across(kvs, row, xs, xr, delta) for delta in (1, 2, 3)}
    later = {delta: across(lasts, last, ls, lr, delta) for delta in (1, 2, 3)}
    part, rest = (slice(None), slice(None), pl.ds(0, FW)), (slice(None), slice(None), pl.ds(FW, LW))
    query = {delta: across(qs.at[part], q.at[part], qss, qsr, delta) for delta in (1, 2, 3)}
    query_later = {delta: across(qs.at[rest], q.at[rest], rss, rsr, delta) for delta in (1, 2, 3)}
    sent = []

    def up_down(delta):
        for way, (dy, to) in enumerate(((1, below), (-1, above))):
            copy = pltpu.make_async_remote_copy(
                row.at[delta], to.at[delta], ys.at[way, delta], yr.at[way, delta],
                device_id=device(y + dy, x), device_id_type=MESH,
            )
            copy.start()
            sent.append(copy)

    for i, (delta, kind) in enumerate(BLOCKS):
        if kind == 0:
            to = q if delta == 0 else qs

            def put(at, value, delta=delta, to=to):
                to[delta, at, :] = (value * SCALE).astype(jnp.bfloat16)
        else:
            to, rest = (row, last) if delta == 0 else (kvs, lasts)

            def put(at, value, delta=delta, kind=kind, to=to, rest=rest):
                value = value.astype(jnp.bfloat16)
                to[delta, at, pl.ds((kind - 1) * FW, FW)] = value[:, :FW]
                rest[delta, at, pl.ds((kind - 1) * LW, LW)] = value[:, FW:]

        product(i, put)
        if kind == 2:
            if delta == 0:
                up_down(0)
            else:
                first[delta].start()
    first[1].wait()
    up_down(1)
    first[3].wait()
    up_down(3)
    for delta in (1, 3, 2):
        query[delta].start()
    first[2].wait()
    up_down(2)
    for delta in (1, 3, 2):
        later[delta].start()
    for delta in (1, 3, 2):
        query_later[delta].start()
    live = [keep[y * SIDE + (x + SIDE - back) % SIDE] * BLK for back in range(SIDE)]
    low = lax.broadcasted_iota(jnp.int32, (1, 128), 1) < HEAD_DIM
    col = lax.broadcasted_iota(jnp.int32, (1, ROWS), 1)
    ones = jnp.ones((ROWS, 128), jnp.bfloat16)

    def own_row(i, carry):
        d, c = i // (FW // 128), i % (FW // 128)

        @pl.when((d > 0) & (c == 0))
        def _():
            across(qs.at[part], q.at[part], qss, qsr, d).wait()

        at = pl.ds(pl.multiple_of(c * 128, 128), 128)
        value_at = pl.ds(pl.multiple_of(FW + c * 128, 128), 128)
        masks = (low, jnp.logical_not(low))
        query_pair = q[d, :, at]
        scores, highest = [], []
        for h in range(2):
            value = jnp.where(masks[h], query_pair, jnp.zeros_like(query_pair))
            rowed = []
            top = None
            for back in range(SIDE):
                score = lax.dot_general(
                    value, row[back, :, at], (((1,), (1,)), ((), ())),
                    preferred_element_type=jnp.float32,
                )
                score = jnp.where(col < live[back], score, -1e30)
                rowed.append(score)
                for t in range(MOSTB):
                    piece = score[:, t * 128 : (t + 1) * 128]
                    top = piece if top is None else jnp.maximum(top, piece)
            scores.append(rowed)
            highest.append(top)
        for h in range(2):
            top = jnp.broadcast_to(jnp.max(highest[h], axis=1, keepdims=True), (ROWS, 128))
            wide = jnp.concatenate([top] * MOSTB, axis=1)
            total = None
            for back in range(SIDE):
                p = jnp.exp2(scores[h][back] - wide).astype(jnp.bfloat16)
                v = jnp.where(masks[h], row[back, :, value_at], ones)
                o = jnp.dot(p, v, preferred_element_type=jnp.float32)
                total = o if total is None else total + o
            tops[d, c, h] = top
            sums[d, c, h] = total
        return carry

    lax.fori_loop(0, SIDE * (FW // 128), own_row, 0)
    for copy in [*later.values(), *query_later.values(), *sent]:
        copy.wait()


def exchange(keep_count, normed, w_qkv):
    dma = pltpu.SemaphoreType.DMA
    vmem = pl.BlockSpec(memory_space=pltpu.VMEM)
    shapes = [(SIDE, ROWS, 2 * FW)] * 3 + [(SIDE, ROWS, 2 * LW), (SIDE, ROWS, GW)]
    return pl.pallas_call(
        exchange_kernel,
        out_shape=[jax.ShapeDtypeStruct(shape, jnp.bfloat16) for shape in shapes]
        + [jax.ShapeDtypeStruct((SIDE, FW // 128, 2, ROWS, 128), jnp.float32)] * 2,
        in_specs=[pl.BlockSpec(memory_space=pltpu.SMEM), vmem, pl.BlockSpec(memory_space=pltpu.HBM)],
        out_specs=[vmem] * 7,
        scratch_shapes=[
            pltpu.VMEM((len(BLOCKS), D, GW), jnp.bfloat16),
            pltpu.VMEM((SIDE, ROWS, 2 * FW), jnp.bfloat16),
            pltpu.VMEM((SIDE, ROWS, 2 * LW), jnp.bfloat16),
            pltpu.VMEM((SIDE, ROWS, GW), jnp.bfloat16),
            dma((len(BLOCKS),)),
            *[dma((SIDE,))] * 8,
            dma((2, SIDE)),
            dma((2, SIDE)),
        ],
        compiler_params=pltpu.CompilerParams(
            collective_id=0, has_side_effects=True, vmem_limit_bytes=36 * 2**20
        ),
        name="exchange",
    )(keep_count, normed, w_qkv)


def attend_kernel(start, pairs, begun, keep, q, *refs):
    if begun:
        below, above, tops, sums = refs[:4]
        sources = ((0, below), (2, above))
    else:
        below, row, above = refs[:3]
        sources = ((0, below), (1, row), (2, above))
    out, live, keys, vals, masked, s0, s1, m0, m1, acc = refs[4 if begun else 3 :]
    y, x = place()
    for k, (dy, _) in enumerate(sources):
        for frame in range(SIDE):
            live[k * SIDE + frame] = keep[((y + SIDE - 1 + dy) % SIDE) * SIDE + frame]
    low = lax.broadcasted_iota(jnp.int32, (1, 128), 1) < HEAD_DIM
    one = jnp.ones((BLK, 128), jnp.bfloat16)
    counts = live
    total = 0
    for k, (_, kv) in enumerate(sources):

        def pack(slot, at, k=k, kv=kv):
            frame, block = slot // MOSTB, slot % MOSTB
            back = (x + SIDE - frame) % SIDE
            used = block < counts[k * SIDE + frame]

            @pl.when(used)
            def _():
                rows = pl.ds(pl.multiple_of(block * BLK, BLK), BLK)
                to = pl.ds(pl.multiple_of(at * BLK, BLK), BLK)
                for c in range(pairs):
                    keys[c, to, :] = kv[back, rows, c * 128 : (c + 1) * 128]
                    v = kv[back, rows, (pairs + c) * 128 : (pairs + c + 1) * 128]
                    vals[c, 0, to, :] = jnp.where(low, v, one)
                    vals[c, 1, to, :] = jnp.where(low, one, v)

            return at + used.astype(jnp.int32)

        total = lax.fori_loop(0, SIDE * MOSTB, pack, total)
    tail = pl.ds(pl.multiple_of(total * BLK, BLK), CH)
    for c in range(pairs):
        keys[c, tail, :] = jnp.zeros((CH, 128), jnp.bfloat16)
        for h in range(2):
            vals[c, h, tail, :] = jnp.zeros((CH, 128), jnp.bfloat16)

    def frame_rows(d, first, blocks, rows):
        full, left = blocks // (CH // BLK), blocks % (CH // BLK)
        for c in range(pairs):
            value = q[d, 0:rows, (start + c) * 128 : (start + c + 1) * 128]
            zero = jnp.zeros_like(value)
            masked[2 * c, 0:rows, :] = jnp.where(low, value, zero)
            masked[2 * c + 1, 0:rows, :] = jnp.where(low, zero, value)

        def span(j, width):
            return (
                pl.ds(pl.multiple_of(first * BLK + j * CH, BLK), width),
                pl.ds(pl.multiple_of(j * CH, BLK), width),
            )

        def score(c, j, width, partial, s, m):
            at, cols = span(j, width)
            for h in range(2):
                value = lax.dot_general(
                    masked[2 * c + h, 0:rows, :], keys[c, at, :],
                    (((1,), (1,)), ((), ())), preferred_element_type=jnp.float32,
                )
                if partial:
                    col = lax.broadcasted_iota(jnp.int32, (1, width), 1)
                    value = jnp.where(col < left * BLK, value, -1e30)
                s[h, 0:rows, cols] = value
                top = m[h, 0:rows, :]
                for t in range(width // 128):
                    top = jnp.maximum(top, value[:, t * 128 : (t + 1) * 128])
                m[h, 0:rows, :] = top

        def weigh(c, j, width, s, m):
            at, cols = span(j, width)
            for h in range(2):
                top = jnp.concatenate([m[h, 0:rows, :]] * (width // 128), axis=1)
                p = jnp.exp2(s[h, 0:rows, cols] - top).astype(jnp.bfloat16)
                acc[h, 0:rows, :] += jnp.dot(p, vals[c, h, at, :], preferred_element_type=jnp.float32)

        bufs = ((s0, m0), (s1, m1))
        for stage in range(pairs + 1):
            s, m = bufs[(stage + 1) % 2]
            sn, mn = bufs[stage % 2]
            if stage:
                top = jnp.broadcast_to(
                    jnp.max(m[:, 0:rows, :], axis=2, keepdims=True), (2, rows, 128)
                )
                if begun:
                    before = tops[d, stage - 1, :, 0:rows, :]
                    top = jnp.maximum(top, before)
                    acc[:, 0:rows, :] = sums[d, stage - 1, :, 0:rows, :] * jnp.exp2(before - top)
                else:
                    acc[:, 0:rows, :] = jnp.zeros((2, rows, 128), jnp.float32)
                m[:, 0:rows, :] = top
            if stage < pairs:
                mn[:, 0:rows, :] = jnp.full((2, rows, 128), -1e30, jnp.float32)

            def step(j, width, partial, stage=stage, s=s, m=m, sn=sn, mn=mn):
                if stage < pairs:
                    score(stage, j, width, partial, sn, mn)
                if stage:
                    weigh(stage - 1, j, width, s, m)

            lax.fori_loop(0, full, lambda j, t, step=step: (step(j, CH, False), t)[1], 0)

            @pl.when((left > 0) & (left <= CH // BLK // 2))
            def _(step=step):
                step(full, CH // 2, True)

            @pl.when(left > CH // BLK // 2)
            def _(step=step):
                step(full, CH, True)

            if stage:
                even, odd = acc[0, 0:rows, :], acc[1, 0:rows, :]
                even = even / pltpu.roll(even, HEAD_DIM, 1)
                odd = odd / pltpu.roll(odd, HEAD_DIM, 1)
                out[d, 0:rows, (stage - 1) * 128 : stage * 128] = jnp.where(low, even, odd).astype(jnp.bfloat16)

    def frame_body(f, first):
        blocks = counts[f]
        for k in range(1, len(sources) * SIDE - SIDE + 1):
            blocks += counts[f + k]
        own = keep[y * SIDE + f]
        d = (x + SIDE - f) % SIDE
        for n in range(1, MOSTB + 1):

            @pl.when(own == n)
            def _(n=n):
                frame_rows(d, first, blocks, n * BLK)
                if n < MOSTB:
                    out[d, n * BLK :, :] = jnp.zeros((ROWS - n * BLK, pairs * 128), jnp.bfloat16)

        return first + counts[f]

    lax.fori_loop(0, SIDE, frame_body, 0)


def attend(start, pairs, begun, keep_count, q, *rest):
    window = BEGUN_WINDOW if begun else WINDOW
    vmem = pl.BlockSpec(memory_space=pltpu.VMEM)
    return pl.pallas_call(
        functools.partial(attend_kernel, start, pairs, begun),
        out_shape=jax.ShapeDtypeStruct((SIDE, ROWS, pairs * 128), jnp.bfloat16),
        in_specs=[pl.BlockSpec(memory_space=pltpu.SMEM)] + [vmem] * (1 + len(rest)),
        out_specs=vmem,
        scratch_shapes=[
            pltpu.SMEM((3 * SIDE,), jnp.int32),
            pltpu.VMEM((pairs, KROWS, 128), jnp.bfloat16),
            pltpu.VMEM((pairs, 2, KROWS, 128), jnp.bfloat16),
            pltpu.VMEM((2 * pairs, ROWS, 128), jnp.bfloat16),
            pltpu.VMEM((2, ROWS, window), jnp.float32),
            pltpu.VMEM((2, ROWS, window), jnp.float32),
            *[pltpu.VMEM((2, ROWS, 128), jnp.float32)] * 3,
        ],
        compiler_params=pltpu.CompilerParams(vmem_limit_bytes=(32 if begun else 36) * 2**20),
        cost_estimate=pl.CostEstimate(
            flops=pairs * 18 * 10**9, bytes_accessed=pairs * 2**21, transcendentals=0
        ),
        name="attend",
    )(keep_count, q, *rest)


def project_kernel(own, one, two, three, rest, w, out, got, wbuf, total, wsem, ss, rs):
    y, x = place()
    order = (0, 1, 3, 2)
    loads = []
    for i, delta in enumerate(order):
        row = pl.multiple_of(((x - delta) % SIDE) * GW, GW)
        load = pltpu.make_async_copy(w.at[pl.ds(row, GW), :], wbuf.at[i], wsem.at[i])
        load.start()
        loads.append(load)
    barrier = pltpu.get_barrier_semaphore()
    for delta in (1, 2, 3):
        pl.semaphore_signal(barrier, inc=1, device_id=device(y, x + delta), device_id_type=MESH)
    pl.semaphore_wait(barrier, 3)
    copies = {}
    for delta in (2, 1, 3):
        copies[delta] = pltpu.make_async_remote_copy(
            rest.at[(SIDE - delta) % SIDE], got.at[delta], ss.at[delta], rs.at[delta],
            device_id=device(y, x + delta), device_id_type=MESH,
        )
        copies[delta].start()
    parts = (own, one, two, three)
    for i, delta in enumerate(order):
        loads[i].wait()

        def first(r, carry, i=i, delta=delta):
            at = pl.ds(pl.multiple_of(r * BLK, BLK), BLK)
            value = jnp.dot(parts[delta][at, :], wbuf[i, :FW, :], preferred_element_type=jnp.float32)
            if i == 0:
                value += jnp.dot(rest[0, at, :], wbuf[i, FW:, :], preferred_element_type=jnp.float32)
            else:
                value += total[at, :]
            total[at, :] = value
            return carry

        lax.fori_loop(0, MOSTB, first, 0)
    for i, delta in enumerate(order):
        if delta == 0:
            continue
        copies[delta].wait()

        def rows(r, carry, i=i, delta=delta):
            at = pl.ds(pl.multiple_of(r * BLK, BLK), BLK)
            value = total[at, :]
            value += jnp.dot(got[delta, at, :], wbuf[i, FW:, :], preferred_element_type=jnp.float32)
            if i < SIDE - 1:
                total[at, :] = value
            else:
                scale = lax.rsqrt(jnp.mean(value * value, axis=-1, keepdims=True) + 1e-06)
                out[at, :] = (value * scale).astype(jnp.bfloat16)
            return carry

        lax.fori_loop(0, MOSTB, rows, 0)


def project(parts, rest, w_out):
    dma = pltpu.SemaphoreType.DMA
    vmem = pl.BlockSpec(memory_space=pltpu.VMEM)
    return pl.pallas_call(
        project_kernel,
        out_shape=jax.ShapeDtypeStruct((ROWS, D), jnp.bfloat16),
        in_specs=[vmem] * 5 + [pl.BlockSpec(memory_space=pltpu.HBM)],
        out_specs=vmem,
        scratch_shapes=[
            pltpu.VMEM((SIDE, ROWS, LW), jnp.bfloat16),
            pltpu.VMEM((SIDE, GW, D), jnp.bfloat16),
            pltpu.VMEM((ROWS, D), jnp.float32),
            *[dma((SIDE,))] * 3,
        ],
        compiler_params=pltpu.CompilerParams(
            collective_id=1, has_side_effects=True, vmem_limit_bytes=24 * 2**20
        ),
        name="project",
    )(*parts, rest, w_out)


def scatter_kernel(order, count, block, out, zero, sems):
    own = count[lax.axis_index("frame")]
    zero[...] = jnp.zeros_like(zero)

    def each(act):
        for j in range(order.shape[1]):
            rows = pl.ds(pl.multiple_of(order[0, j] * BLK, BLK), BLK)
            if j == MOSTB:
                act(pltpu.make_async_copy(zero, out.at[rows, :], sems.at[j]))
                continue

            @pl.when(j < own)
            def _(j=j, rows=rows):
                act(pltpu.make_async_copy(block.at[pl.ds(j * BLK, BLK), :], out.at[rows, :], sems.at[j]))

            @pl.when(j >= own)
            def _(j=j, rows=rows):
                act(pltpu.make_async_copy(zero, out.at[rows, :], sems.at[j]))

    each(lambda copy: copy.start())
    each(lambda copy: copy.wait())


def scatter(keep_order, keep_count, normalized):
    blocks = keep_order.shape[1]
    smem = pl.BlockSpec(memory_space=pltpu.SMEM)
    return pl.pallas_call(
        scatter_kernel,
        in_specs=[smem, smem, pl.BlockSpec(memory_space=pltpu.VMEM)],
        out_specs=pl.BlockSpec(memory_space=pl.ANY),
        out_shape=jax.ShapeDtypeStruct((blocks * BLK, D), jnp.bfloat16),
        scratch_shapes=[pltpu.VMEM((BLK, D), jnp.bfloat16), pltpu.SemaphoreType.DMA((blocks,))],
        compiler_params=pltpu.CompilerParams(vmem_limit_bytes=8 * 2**20),
        name="scatter",
    )(keep_order, keep_count, normalized)


def shifted(value, dy, dx):
    def to(f):
        return (f // SIDE + dy) % SIDE * SIDE + (f + dx) % SIDE

    return lax.ppermute(value, "frame", [(f, to(f)) for f in range(SIDE * SIDE)])


def shards(tokens, keep_count, keep_order, w_qkv, w_out):
    normed = norm_kept(keep_order, tokens)
    below, row, above, last, q, tops, sums = exchange(keep_count, normed, w_qkv)
    last_below = shifted(last, 1, 0)
    last_above = shifted(last, -1, 0)
    part = attend(0, 2, True, keep_count, q, below, above, tops, sums)
    parts = [shifted(part[(SIDE - dx) % SIDE], 0, dx) if dx else part[0] for dx in range(SIDE)]
    rest = attend(2, 1, False, keep_count, q, last_below, last, last_above)
    normalized = project(parts, rest, w_out)
    return scatter(keep_order, keep_count, normalized)


def solution(mesh):
    return jax.shard_map(
        shards,
        mesh=mesh,
        in_specs=(P(("orbit", "frame"), None), P("orbit"), P(("orbit", "frame"), None), P(), P()),
        out_specs=P(("orbit", "frame"), None),
        check_vma=False,
    )
```

profile of v0, /device:TPU:64, one launch (start us, length us, event | category | flops | bytes accessed | tf_op | source)
XLA Modules:
  0.0 106.6 jit_solution(3568979531042563902)
XLA Ops:
  0.0 1.4 %copy-done = bf16[512,1536]{1,0:T(8,128)(2,1)S(1)} copy-done((bf16[512,1536]{1,0:T(8,128)(2,1)S(1)}, bf16[512,1536]{1,0:T(8,128)(2,1)}, u32[]{:S(2)}) %copy-start) | copy-done | bytes 1572888
  1.4 0.7 copy-done.2
  2.1 1.6 %norm_kept.1.normed = bf16[384,1536]{1,0:T(8,128)(2,1)S(1)} custom-call(s32[1,4]{1,0:T(1,128)S(1)} %copy-done.2, bf16[512,1536]{1,0:T(8,128)(2,1)S(1)} %copy-done), custom_call_target="tpu_custom_call" | custom-call | tf_op jit(solution)/shard_map/norm_kept/pallas_call | solution.py:49
  3.7 0.0 copy-done.1
  3.7 0.0 slice-start
  3.7 51.0 %exchange.1 = (bf16[4,384,512]{2,1,0:T(8,128)(2,1)S(1)}, bf16[4,384,512]{2,1,0:T(8,128)(2,1)}, bf16[4,384,512]{2,1,0:T(8,128)(2,1)S(1)}, bf16[4,384,256]{2,1,0:T...) custom-call(s32[16]{0:T(128)S(1)} %copy-done.1, ...), custom_call_target="tpu_custom_call" | custom-call | tf_op jit(solution)/shard_map/exchange/pallas_call | solution.py:202
  54.8 3.4 %collective-permute-start.4 = (bf16[4,384,256]{2,1,0:T(8,128)(2,1)S(1)}, bf16[4,384,256]{2,1,0:T(8,128)(2,1)S(1)}, u32[]{:S(2)}, u32[]{:S(2)}) collective-permute-start(bf16[4,384,256]{2,1,0:T(8,128)(2,1)S(1)} %get-tuple-element.16.refs_1_), channel_id=1, source_target_pairs={{0,96},{8,104},{16,112},{24,120},{32,0},{40,8},{48,16},{56,24},{64... | collective-permute-start | bytes 2359304 | tf_op jit(solution)/shard_map/ppermute | solution.py:504
  58.2 0.0 collective-permute-start.3
  58.2 15.3 %attend.2 = bf16[4,384,256]{2,1,0:T(8,128)(2,1)S(1)} custom-call(s32[16]{0:T(128)S(1)} %copy-done.1, bf16[4,384,384]{2,1,0:T(8,128)(2,1)S(1)} %get-tuple-element.11.q, bf16[4,384,512]{2,1,0:T(8,128)(2,1)S(1)} %get-tuple-element.12.refs_0_, bf16[4,384,512]{2,1,0:T(8,128)(2,1)S(1)} %get-tuple-element.13.refs_1_, ...), custom_call_target="tpu_custom_call" | custom-call | flops 35999997952 | bytes 4194304 | tf_op jit(solution)/shard_map/attend/pallas_call | solution.py:366
  73.5 0.1 slice_bitcast_fusion
  73.6 2.6 %collective-permute-start.2 = (bf16[384,256]{1,0:T(8,128)(2,1)S(1)}, bf16[384,256]{1,0:T(8,128)(2,1)S(1)}, u32[]{:S(2)}, u32[]{:S(2)}) collective-permute-start(bf16[384,256]{1,0:T(8,128)(2,1)S(1)} %get-tuple-element.17), channel_id=1, source_target_pairs={{0,24},{8,0},{16,8},{24,16},{32,56},{40,32},{48,40},{56,48},{64,88... | collective-permute-start | bytes 589832 | tf_op jit(solution)/shard_map/ppermute | solution.py:504
  76.2 1.4 %collective-permute-start.1 = (bf16[384,256]{1,0:T(8,128)(2,1)S(1)}, bf16[384,256]{1,0:T(8,128)(2,1)S(1)}, u32[]{:S(2)}, u32[]{:S(2)}) collective-permute-start(bf16[384,256]{1,0:T(8,128)(2,1)S(1)} %get-tuple-element.18), channel_id=1, source_target_pairs={{0,16},{8,24},{16,0},{24,8},{32,48},{40,56},{48,32},{56,40},{64,80... | collective-permute-start | bytes 589832 | tf_op jit(solution)/shard_map/ppermute | solution.py:504
  77.6 0.0 collective-permute-start
  77.6 0.0 collective-permute-done.4.refs_2_
  77.6 0.0 collective-permute-done.3.refs_0_
  77.6 12.8 %attend.3.rest = bf16[4,384,128]{2,1,0:T(8,128)(2,1)S(1)} custom-call(s32[16]{0:T(128)S(1)} %copy-done.1, bf16[4,384,384]{2,1,0:T(8,128)(2,1)S(1)} %get-tuple-element.11.q, bf16[4,384,256]{2,1,0:T(8,128)(2,1)S(1)} %collective-permute-done.3.refs_0_, bf16[4,384,256]{2,1,0:T(8,128)(2,1)S(1)} %get-tuple-element.16.refs_1_, ...), custom_call_target="tpu_custom_call" | custom-call | flops 17999998976 | bytes 2097152 | tf_op jit(solution)/shard_map/attend/pallas_call | solution.py:366
  90.4 0.0 collective-permute-done.2.three
  90.5 0.0 collective-permute-done.1.two
  90.5 0.0 collective-permute-done.one
  90.5 0.0 slice-done
  90.5 0.0 slice-done.1
  90.5 0.0 copy-start.3
  90.5 14.2 %project.1.block = bf16[384,1536]{1,0:T(8,128)(2,1)S(1)} custom-call(bf16[384,256]{1,0:T(8,128)(2,1)S(1)} %get-tuple-element.20.own, bf16[384,256]{1,0:T(8,128)(2,1)S(1)} %collective-permute-done.one, bf16[384,256]{1,0:T(8,128)(2,1)S(1)} %collective-permute-done.1.two, bf16[384,256]{1,0:T(8,128)(2,1)S(1)} %collective-permute-done.2.three, ...), custom_call_target="tpu_custom_call" | custom-call | tf_op jit(solution)/shard_map/project/pallas_call | solution.py:445
  104.7 1.7 %scatter.1 = bf16[512,1536]{1,0:T(8,128)(2,1)} custom-call(s32[1,4]{1,0:T(1,128)S(1)} %copy-done.3, s32[16]{0:T(128)S(1)} %copy-done.1, bf16[384,1536]{1,0:T(8,128)(2,1)S(1)} %project.1.block), custom_call_target="tpu_custom_call" | custom-call | tf_op jit(solution)/shard_map/scatter/pallas_call | solution.py:489
  (6 shorter events, 0.0 us)
Async XLA Ops:
  0.0 1.4 %copy-start = (bf16[512,1536]{1,0:T(8,128)(2,1)S(1)}, bf16[512,1536]{1,0:T(8,128)(2,1)}, u32[]{:S(2)}) copy-start(bf16[512,1536]{1,0:T(8,128)(2,1)} %tokens.1) | copy-start | bytes 4718596
  1.4 0.7 copy-start.2
  2.1 1.7 %copy-start.1 = (s32[16]{0:T(128)S(1)}, s32[16]{0:T(128)}, u32[]{:S(2)}) copy-start(s32[16]{0:T(128)} %count.1) | copy-start | bytes 196
  3.7 86.7 %slice-start = ((s8[4718592]{0:T(1024)(128)(4,1)}), s8[524288]{0:T(1024)(128)(4,1)S(1)}, s32[]{:S(2)}) async-start(s8[4718592]{0:T(1024)(128)(4,1)} %bitcast.8), calls=%async_computation | async-start | bytes 1048576
  54.8 22.8 %collective-permute-start.4 = (bf16[4,384,256]{2,1,0:T(8,128)(2,1)S(1)}, bf16[4,384,256]{2,1,0:T(8,128)(2,1)S(1)}, u32[]{:S(2)}, u32[]{:S(2)}) collective-permute-start(bf16[4,384,256]{2,1,0:T(8,128)(2,1)S(1)} %get-tuple-element.16.refs_1_), channel_id=1, source_target_pairs={{0,96},{8,104},{16,112},{24,120},{32,0},{40,8},{48,16},{56,24},{64... | collective-permute-start | bytes 2359304 | tf_op jit(solution)/shard_map/ppermute | solution.py:504
  58.2 19.4 %collective-permute-start.3 = (bf16[4,384,256]{2,1,0:T(8,128)(2,1)S(1)}, bf16[4,384,256]{2,1,0:T(8,128)(2,1)S(1)}, u32[]{:S(2)}, u32[]{:S(2)}) collective-permute-start(bf16[4,384,256]{2,1,0:T(8,128)(2,1)S(1)} %get-tuple-element.16.refs_1_), channel_id=1, source_target_pairs={{0,32},{8,40},{16,48},{24,56},{32,64},{40,72},{48,80},{56,88},{64,... | collective-permute-start | bytes 2359304 | tf_op jit(solution)/shard_map/ppermute | solution.py:504
  58.2 32.3 %slice-start.1 = ((s8[4718592]{0:T(1024)(128)(4,1)}), s8[4194304]{0:T(1024)(128)(4,1)S(1)}, s32[]{:S(2)}) async-start(s8[4718592]{0:T(1024)(128)(4,1)} %bitcast.8), calls=%async_computation.1 | async-start | bytes 8388608
  73.6 16.9 %collective-permute-start.2 = (bf16[384,256]{1,0:T(8,128)(2,1)S(1)}, bf16[384,256]{1,0:T(8,128)(2,1)S(1)}, u32[]{:S(2)}, u32[]{:S(2)}) collective-permute-start(bf16[384,256]{1,0:T(8,128)(2,1)S(1)} %get-tuple-element.17), channel_id=1, source_target_pairs={{0,24},{8,0},{16,8},{24,16},{32,56},{40,32},{48,40},{56,48},{64,88... | collective-permute-start | bytes 589832 | tf_op jit(solution)/shard_map/ppermute | solution.py:504
  76.2 14.3 %collective-permute-start.1 = (bf16[384,256]{1,0:T(8,128)(2,1)S(1)}, bf16[384,256]{1,0:T(8,128)(2,1)S(1)}, u32[]{:S(2)}, u32[]{:S(2)}) collective-permute-start(bf16[384,256]{1,0:T(8,128)(2,1)S(1)} %get-tuple-element.18), channel_id=1, source_target_pairs={{0,16},{8,24},{16,0},{24,8},{32,48},{40,56},{48,32},{56,40},{64,80... | collective-permute-start | bytes 589832 | tf_op jit(solution)/shard_map/ppermute | solution.py:504
  77.6 12.9 %collective-permute-start = (bf16[384,256]{1,0:T(8,128)(2,1)S(1)}, bf16[384,256]{1,0:T(8,128)(2,1)S(1)}, u32[]{:S(2)}, u32[]{:S(2)}) collective-permute-start(bf16[384,256]{1,0:T(8,128)(2,1)S(1)} %get-tuple-element.19), channel_id=1, source_target_pairs={{0,8},{8,16},{16,24},{24,0},{32,40},{40,48},{48,56},{56,32},{64,72... | collective-permute-start | bytes 589832 | tf_op jit(solution)/shard_map/ppermute | solution.py:504
  90.5 14.2 %copy-start.3 = (s32[1,4]{1,0:T(1,128)S(1)}, s32[1,4]{1,0:T(1,128)}, u32[]{:S(2)}) copy-start(s32[1,4]{1,0:T(1,128)} %order.3) | copy-start | bytes 52
where the time goes:
time: 108 us; the launch traced here: 107 us
  Pallas kernels  96.7 us (90%)
  starting transfers between devices  7.42 us (7%)
  local copies, waits for them, and re-layouts  2.14 us (2%)
    pallas_call x1, Pallas kernels, exchange(): pl.pallas_call(exchange_kernel, out_shape=[jax.ShapeDtypeStruct(shape, jn...  51 us
    pallas_call x2, Pallas kernels, attend(): pl.pallas_call(functools.partial(attend_kernel, start, pairs, begun), out...  28.2 us
    pallas_call x1, Pallas kernels, project(): pl.pallas_call(project_kernel, out_shape=jax.ShapeDtypeStruct((ROWS, D),...  14.2 us
    ppermute x5, starting transfers between devices, shifted(): lax.ppermute(value, 'frame', [(f, to(f)) for f in range(SIDE * SIDE)])  7.42 us
  transfers between devices with their start and end apart: 5, of which 0 were waited for; matrix products, arithmetic and copies ran while one was open for 0% of the time, Pallas kernels for 26%

commit v1 on v0

--- a/solution.py
+++ b/solution.py
@@ -77,7 +77,6 @@
     peers = [(0, 1), (0, 2), (0, 3), (1, 0), (3, 0)]
     for dy, dx in peers:
         pl.semaphore_signal(barrier, inc=1, device_id=device(y + dy, x + dx), device_id_type=MESH)
-    pl.semaphore_wait(barrier, len(peers))
 
     def product(i, put):
         loads[i].wait()
@@ -127,6 +126,8 @@
                 rest[delta, at, pl.ds((kind - 1) * LW, LW)] = value[:, FW:]
 
         product(i, put)
+        if i == 1:
+            pl.semaphore_wait(barrier, len(peers))
         if kind == 2:
             if delta == 0:
                 up_down(0)
@@ -385,58 +386,59 @@
     )(keep_count, q, *rest)
 
 
-def project_kernel(own, one, two, three, rest, w, out, got, wbuf, total, wsem, ss, rs):
+def project_kernel(own, one, two, three, rest, w, out, got, most, few, total, wsem, ss, rs):
     y, x = place()
-    order = (0, 1, 3, 2)
-    loads = []
-    for i, delta in enumerate(order):
-        row = pl.multiple_of(((x - delta) % SIDE) * GW, GW)
-        load = pltpu.make_async_copy(w.at[pl.ds(row, GW), :], wbuf.at[i], wsem.at[i])
-        load.start()
-        loads.append(load)
     barrier = pltpu.get_barrier_semaphore()
     for delta in (1, 2, 3):
         pl.semaphore_signal(barrier, inc=1, device_id=device(y, x + delta), device_id_type=MESH)
+    loads = []
+    for delta in range(SIDE):
+        group = ((x + SIDE - delta) % SIDE) * GW
+        for k, (skip, size, to) in enumerate(((0, FW, most), (FW, LW, few))):
+            rows = pl.ds(pl.multiple_of(group + skip, LW), size)
+            load = pltpu.make_async_copy(w.at[rows, :], to.at[pl.ds(delta * size, size), :], wsem.at[k, delta])
+            load.start()
+            loads.append(load)
     pl.semaphore_wait(barrier, 3)
-    copies = {}
+    copies = []
     for delta in (2, 1, 3):
-        copies[delta] = pltpu.make_async_remote_copy(
+        copy = pltpu.make_async_remote_copy(
             rest.at[(SIDE - delta) % SIDE], got.at[delta], ss.at[delta], rs.at[delta],
             device_id=device(y, x + delta), device_id_type=MESH,
         )
-        copies[delta].start()
-    parts = (own, one, two, three)
-    for i, delta in enumerate(order):
-        loads[i].wait()
-
-        def first(r, carry, i=i, delta=delta):
-            at = pl.ds(pl.multiple_of(r * BLK, BLK), BLK)
-            value = jnp.dot(parts[delta][at, :], wbuf[i, :FW, :], preferred_element_type=jnp.float32)
-            if i == 0:
-                value += jnp.dot(rest[0, at, :], wbuf[i, FW:, :], preferred_element_type=jnp.float32)
-            else:
-                value += total[at, :]
-            total[at, :] = value
-            return carry
-
-        lax.fori_loop(0, MOSTB, first, 0)
-    for i, delta in enumerate(order):
-        if delta == 0:
-            continue
-        copies[delta].wait()
-
-        def rows(r, carry, i=i, delta=delta):
-            at = pl.ds(pl.multiple_of(r * BLK, BLK), BLK)
-            value = total[at, :]
-            value += jnp.dot(got[delta, at, :], wbuf[i, FW:, :], preferred_element_type=jnp.float32)
-            if i < SIDE - 1:
-                total[at, :] = value
-            else:
-                scale = lax.rsqrt(jnp.mean(value * value, axis=-1, keepdims=True) + 1e-06)
-                out[at, :] = (value * scale).astype(jnp.bfloat16)
-            return carry
-
-        lax.fori_loop(0, MOSTB, rows, 0)
+        copy.start()
+        copies.append(copy)
+    for load in loads:
+        load.wait()
+    tile = 512
+
+    def first(t, carry):
+        cols = pl.ds(pl.multiple_of(t * tile, 128), tile)
+        left = jnp.concatenate([own[...], one[...], two[...], three[...], rest[0]], axis=1)
+        right = jnp.concatenate([most[:, cols], few[0:LW, cols]], axis=0)
+        total[:, cols] = jnp.dot(left, right, preferred_element_type=jnp.float32)
+        return carry
+
+    lax.fori_loop(0, D // tile, first, 0)
+    for copy in copies:
+        copy.wait()
+
+    def second(t, square):
+        cols = pl.ds(pl.multiple_of(t * tile, 128), tile)
+        left = jnp.concatenate([got[1], got[2], got[3]], axis=1)
+        value = total[:, cols] + jnp.dot(left, few[LW:, cols], preferred_element_type=jnp.float32)
+        total[:, cols] = value
+        for k in range(tile // 128):
+            piece = value[:, k * 128 : (k + 1) * 128]
+            square += piece * piece
+        return square
+
+    square = lax.fori_loop(0, D // tile, second, jnp.zeros((ROWS, 128), jnp.float32))
+    scale = lax.rsqrt(jnp.sum(square, axis=1, keepdims=True) / D + 1e-06)
+    scale = jnp.broadcast_to(scale, (ROWS, 128))
+    for k in range(D // 128):
+        cols = slice(k * 128, (k + 1) * 128)
+        out[:, cols] = (total[:, cols] * scale).astype(jnp.bfloat16)
 
 
 def project(parts, rest, w_out):
@@ -449,9 +451,12 @@
         out_specs=vmem,
         scratch_shapes=[
             pltpu.VMEM((SIDE, ROWS, LW), jnp.bfloat16),
-            pltpu.VMEM((SIDE, GW, D), jnp.bfloat16),
+            pltpu.VMEM((SIDE * FW, D), jnp.bfloat16),
+            pltpu.VMEM((SIDE * LW, D), jnp.bfloat16),
             pltpu.VMEM((ROWS, D), jnp.float32),
-            *[dma((SIDE,))] * 3,
+            dma((2, SIDE)),
+            dma((SIDE,)),
+            dma((SIDE,)),
         ],
         compiler_params=pltpu.CompilerParams(
             collective_id=1, has_side_effects=True, vmem_limit_bytes=24 * 2**20

time: 108 us -> 105 us (0.972)
  Pallas kernels: 96.7 us -> 91.9 us
  starting transfers between devices: 7.42 us -> 8.64 us
    pallas_call x1, Pallas kernels: 14.2 us -> 11.5 us  [project(): pl.pallas_call(project_kernel, out_shape=jax.ShapeDtypeStruct((ROWS, D),...]
    pallas_call x1, Pallas kernels: 51 us -> 49.3 us  [exchange(): pl.pallas_call(exchange_kernel, out_shape=[jax.ShapeDtypeStruct(shape, jn...]
    ppermute x5, starting transfers between devices: 7.42 us -> 8.64 us  [shifted(): lax.ppermute(value, 'frame', [(f, to(f)) for f in range(SIDE * SIDE)])]
  transfers between devices with their start and end apart: 5 -> 5, of which waited for: 0 -> 0; matrix products, arithmetic and copies ran while one was open for 0% -> 0% of each run, Pallas kernels for 26% -> 27%
where the time goes in v1:
time: 105 us; the launch traced here: 103 us
  Pallas kernels  91.9 us (88%)
  starting transfers between devices  8.64 us (8%)
  local copies, waits for them, and re-layouts  2.14 us (2%)
    pallas_call x1, Pallas kernels, exchange(): pl.pallas_call(exchange_kernel, out_shape=[jax.ShapeDtypeStruct(shape, jn...  49.3 us
    pallas_call x2, Pallas kernels, attend(): pl.pallas_call(functools.partial(attend_kernel, start, pairs, begun), out...  27.8 us
    pallas_call x1, Pallas kernels, project(): pl.pallas_call(project_kernel, out_shape=jax.ShapeDtypeStruct((ROWS, D),...  11.5 us
    ppermute x5, starting transfers between devices, shifted(): lax.ppermute(value, 'frame', [(f, to(f)) for f in range(SIDE * SIDE)])  8.64 us
  transfers between devices with their start and end apart: 5, of which 0 were waited for; matrix products, arithmetic and copies ran while one was open for 0% of the time, Pallas kernels for 27%

profile of v1, /device:TPU:64, one launch (start us, length us, event | category | flops | bytes accessed | tf_op | source)
XLA Modules:
  0.0 103.0 jit_solution(7753634842320607465)
XLA Ops:
  0.0 1.4 %copy-done = bf16[512,1536]{1,0:T(8,128)(2,1)S(1)} copy-done((bf16[512,1536]{1,0:T(8,128)(2,1)S(1)}, bf16[512,1536]{1,0:T(8,128)(2,1)}, u32[]{:S(2)}) %copy-start) | copy-done | bytes 1572888
  1.4 0.7 copy-done.2
  2.1 1.6 %norm_kept.1.normed = bf16[384,1536]{1,0:T(8,128)(2,1)S(1)} custom-call(s32[1,4]{1,0:T(1,128)S(1)} %copy-done.2, bf16[512,1536]{1,0:T(8,128)(2,1)S(1)} %copy-done), custom_call_target="tpu_custom_call" | custom-call | tf_op jit(solution)/shard_map/norm_kept/pallas_call | solution.py:49
  3.7 0.0 copy-done.1
  3.7 0.0 slice-start
  3.7 49.3 %exchange.1 = (bf16[4,384,512]{2,1,0:T(8,128)(2,1)S(1)}, bf16[4,384,512]{2,1,0:T(8,128)(2,1)}, bf16[4,384,512]{2,1,0:T(8,128)(2,1)S(1)}, bf16[4,384,256]{2,1,0:T...) custom-call(s32[16]{0:T(128)S(1)} %copy-done.1, ...), custom_call_target="tpu_custom_call" | custom-call | tf_op jit(solution)/shard_map/exchange/pallas_call | solution.py:203
  53.0 3.1 %collective-permute-start.4 = (bf16[4,384,256]{2,1,0:T(8,128)(2,1)S(1)}, bf16[4,384,256]{2,1,0:T(8,128)(2,1)S(1)}, u32[]{:S(2)}, u32[]{:S(2)}) collective-permute-start(bf16[4,384,256]{2,1,0:T(8,128)(2,1)S(1)} %get-tuple-element.16.refs_1_), channel_id=1, source_target_pairs={{0,96},{8,104},{16,112},{24,120},{32,0},{40,8},{48,16},{56,24},{64... | collective-permute-start | bytes 2359304 | tf_op jit(solution)/shard_map/ppermute | solution.py:509
  56.1 0.0 collective-permute-start.3
  56.1 15.7 %attend.2 = bf16[4,384,256]{2,1,0:T(8,128)(2,1)S(1)} custom-call(s32[16]{0:T(128)S(1)} %copy-done.1, bf16[4,384,384]{2,1,0:T(8,128)(2,1)S(1)} %get-tuple-element.11.q, bf16[4,384,512]{2,1,0:T(8,128)(2,1)S(1)} %get-tuple-element.12.refs_0_, bf16[4,384,512]{2,1,0:T(8,128)(2,1)S(1)} %get-tuple-element.13.refs_1_, ...), custom_call_target="tpu_custom_call" | custom-call | flops 35999997952 | bytes 4194304 | tf_op jit(solution)/shard_map/attend/pallas_call | solution.py:367
  71.8 0.1 slice_bitcast_fusion
  71.8 4.0 %collective-permute-start.2 = (bf16[384,256]{1,0:T(8,128)(2,1)S(1)}, bf16[384,256]{1,0:T(8,128)(2,1)S(1)}, u32[]{:S(2)}, u32[]{:S(2)}) collective-permute-start(bf16[384,256]{1,0:T(8,128)(2,1)S(1)} %get-tuple-element.17), channel_id=1, source_target_pairs={{0,24},{8,0},{16,8},{24,16},{32,56},{40,32},{48,40},{56,48},{64,88... | collective-permute-start | bytes 589832 | tf_op jit(solution)/shard_map/ppermute | solution.py:509
  75.9 1.5 %collective-permute-start.1 = (bf16[384,256]{1,0:T(8,128)(2,1)S(1)}, bf16[384,256]{1,0:T(8,128)(2,1)S(1)}, u32[]{:S(2)}, u32[]{:S(2)}) collective-permute-start(bf16[384,256]{1,0:T(8,128)(2,1)S(1)} %get-tuple-element.18), channel_id=1, source_target_pairs={{0,16},{8,24},{16,0},{24,8},{32,48},{40,56},{48,32},{56,40},{64,80... | collective-permute-start | bytes 589832 | tf_op jit(solution)/shard_map/ppermute | solution.py:509
  77.4 0.0 collective-permute-start
  77.4 0.0 collective-permute-done.4.refs_2_
  77.4 0.0 collective-permute-done.3.refs_0_
  77.4 12.2 %attend.3.rest = bf16[4,384,128]{2,1,0:T(8,128)(2,1)S(1)} custom-call(s32[16]{0:T(128)S(1)} %copy-done.1, bf16[4,384,384]{2,1,0:T(8,128)(2,1)S(1)} %get-tuple-element.11.q, bf16[4,384,256]{2,1,0:T(8,128)(2,1)S(1)} %collective-permute-done.3.refs_0_, bf16[4,384,256]{2,1,0:T(8,128)(2,1)S(1)} %get-tuple-element.16.refs_1_, ...), custom_call_target="tpu_custom_call" | custom-call | flops 17999998976 | bytes 2097152 | tf_op jit(solution)/shard_map/attend/pallas_call | solution.py:367
  89.6 0.0 collective-permute-done.2.three
  89.6 0.0 collective-permute-done.1.two
  89.6 0.0 collective-permute-done.one
  89.6 0.0 slice-done
  89.6 0.0 slice-done.1
  89.6 0.0 copy-start.3
  89.6 11.5 %project.1.block = bf16[384,1536]{1,0:T(8,128)(2,1)S(1)} custom-call(bf16[384,256]{1,0:T(8,128)(2,1)S(1)} %get-tuple-element.20.own, bf16[384,256]{1,0:T(8,128)(2,1)S(1)} %collective-permute-done.one, bf16[384,256]{1,0:T(8,128)(2,1)S(1)} %collective-permute-done.1.two, bf16[384,256]{1,0:T(8,128)(2,1)S(1)} %collective-permute-done.2.three, ...), custom_call_target="tpu_custom_call" | custom-call | tf_op jit(solution)/shard_map/project/pallas_call | solution.py:447
  101.1 1.7 %scatter.1 = bf16[512,1536]{1,0:T(8,128)(2,1)} custom-call(s32[1,4]{1,0:T(1,128)S(1)} %copy-done.3, s32[16]{0:T(128)S(1)} %copy-done.1, bf16[384,1536]{1,0:T(8,128)(2,1)S(1)} %project.1.block), custom_call_target="tpu_custom_call" | custom-call | tf_op jit(solution)/shard_map/scatter/pallas_call | solution.py:494
  (6 shorter events, 0.0 us)
Async XLA Ops:
  0.0 1.4 %copy-start = (bf16[512,1536]{1,0:T(8,128)(2,1)S(1)}, bf16[512,1536]{1,0:T(8,128)(2,1)}, u32[]{:S(2)}) copy-start(bf16[512,1536]{1,0:T(8,128)(2,1)} %tokens.1) | copy-start | bytes 4718596
  1.4 0.7 copy-start.2
  2.1 1.7 %copy-start.1 = (s32[16]{0:T(128)S(1)}, s32[16]{0:T(128)}, u32[]{:S(2)}) copy-start(s32[16]{0:T(128)} %count.1) | copy-start | bytes 196
  3.7 85.9 %slice-start = ((s8[4718592]{0:T(1024)(128)(4,1)}), s8[524288]{0:T(1024)(128)(4,1)S(1)}, s32[]{:S(2)}) async-start(s8[4718592]{0:T(1024)(128)(4,1)} %bitcast.8), calls=%async_computation | async-start | bytes 1048576
  53.0 24.4 %collective-permute-start.4 = (bf16[4,384,256]{2,1,0:T(8,128)(2,1)S(1)}, bf16[4,384,256]{2,1,0:T(8,128)(2,1)S(1)}, u32[]{:S(2)}, u32[]{:S(2)}) collective-permute-start(bf16[4,384,256]{2,1,0:T(8,128)(2,1)S(1)} %get-tuple-element.16.refs_1_), channel_id=1, source_target_pairs={{0,96},{8,104},{16,112},{24,120},{32,0},{40,8},{48,16},{56,24},{64... | collective-permute-start | bytes 2359304 | tf_op jit(solution)/shard_map/ppermute | solution.py:509
  56.1 21.3 %collective-permute-start.3 = (bf16[4,384,256]{2,1,0:T(8,128)(2,1)S(1)}, bf16[4,384,256]{2,1,0:T(8,128)(2,1)S(1)}, u32[]{:S(2)}, u32[]{:S(2)}) collective-permute-start(bf16[4,384,256]{2,1,0:T(8,128)(2,1)S(1)} %get-tuple-element.16.refs_1_), channel_id=1, source_target_pairs={{0,32},{8,40},{16,48},{24,56},{32,64},{40,72},{48,80},{56,88},{64,... | collective-permute-start | bytes 2359304 | tf_op jit(solution)/shard_map/ppermute | solution.py:509
  56.1 33.5 %slice-start.1 = ((s8[4718592]{0:T(1024)(128)(4,1)}), s8[4194304]{0:T(1024)(128)(4,1)S(1)}, s32[]{:S(2)}) async-start(s8[4718592]{0:T(1024)(128)(4,1)} %bitcast.8), calls=%async_computation.1 | async-start | bytes 8388608
  71.8 17.7 %collective-permute-start.2 = (bf16[384,256]{1,0:T(8,128)(2,1)S(1)}, bf16[384,256]{1,0:T(8,128)(2,1)S(1)}, u32[]{:S(2)}, u32[]{:S(2)}) collective-permute-start(bf16[384,256]{1,0:T(8,128)(2,1)S(1)} %get-tuple-element.17), channel_id=1, source_target_pairs={{0,24},{8,0},{16,8},{24,16},{32,56},{40,32},{48,40},{56,48},{64,88... | collective-permute-start | bytes 589832 | tf_op jit(solution)/shard_map/ppermute | solution.py:509
  75.9 13.7 %collective-permute-start.1 = (bf16[384,256]{1,0:T(8,128)(2,1)S(1)}, bf16[384,256]{1,0:T(8,128)(2,1)S(1)}, u32[]{:S(2)}, u32[]{:S(2)}) collective-permute-start(bf16[384,256]{1,0:T(8,128)(2,1)S(1)} %get-tuple-element.18), channel_id=1, source_target_pairs={{0,16},{8,24},{16,0},{24,8},{32,48},{40,56},{48,32},{56,40},{64,80... | collective-permute-start | bytes 589832 | tf_op jit(solution)/shard_map/ppermute | solution.py:509
  77.4 12.2 %collective-permute-start = (bf16[384,256]{1,0:T(8,128)(2,1)S(1)}, bf16[384,256]{1,0:T(8,128)(2,1)S(1)}, u32[]{:S(2)}, u32[]{:S(2)}) collective-permute-start(bf16[384,256]{1,0:T(8,128)(2,1)S(1)} %get-tuple-element.19), channel_id=1, source_target_pairs={{0,8},{8,16},{16,24},{24,0},{32,40},{40,48},{48,56},{56,32},{64,72... | collective-permute-start | bytes 589832 | tf_op jit(solution)/shard_map/ppermute | solution.py:509
  89.6 11.5 %copy-start.3 = (s32[1,4]{1,0:T(1,128)S(1)}, s32[1,4]{1,0:T(1,128)}, u32[]{:S(2)}) copy-start(s32[1,4]{1,0:T(1,128)} %order.3) | copy-start | bytes 52
